TPU v7x, 32 devices: a whole 2x2x4 slice. The times are simulated.
32 devices in a mesh: dp: 2 (over core), head: 4 (over y, x), mlp: 4 (over z).
Axes of the slice: x: 2, y: 2, z: 4, core: 2. Of those that a mesh axis runs over, the one named last changes fastest.
Arguments:
- tokens: bfloat16 [2048, 8, 1024], P('head', ('dp', 'mlp')), may hold values from -6 to 6
- first_values: bfloat16 [2048, 8, 1024], P(None, ('dp', 'mlp'), 'head'), may hold values from -10.5 to 10.5
- segment_ids: int32 [2048, 8], P(None, ('dp', 'mlp')), may hold values from 0 to 7, as said below
- positions: int32 [2048, 8], P(None, ('dp', 'mlp')), may hold values from 0 to 2047, as said below
- attn_gain: float32 [1024], replicated, may hold values from 0.5 to 1.5
- w_query: bfloat16 [1024, 1024], P(None, 'head'), may hold values from -0.1875 to 0.1875
- w_key: bfloat16 [1024, 1024], P(None, 'head'), may hold values from -0.1875 to 0.1875
- w_value: bfloat16 [1024, 1024], P(None, 'head'), may hold values from -0.1875 to 0.1875
- w_out: bfloat16 [1024, 1024], P('head'), may hold values from -2 to 2
- mlp_gain: float32 [1024], replicated, may hold values from 0.5 to 1.5
- w_gate: bfloat16 [1024, 2816], P(None, 'mlp'), may hold values from -0.1875 to 0.1875
- w_up: bfloat16 [1024, 2816], P(None, 'mlp'), may hold values from -0.1875 to 0.1875
- w_down: bfloat16 [2816, 1024], P('mlp'), may hold values from -0.109375 to 0.109375
- out_grad: bfloat16 [2048, 8, 1024], P('head', ('dp', 'mlp')), may hold values from -6 to 6
Outputs:
- output: bfloat16 [2048, 8, 1024], P('head', ('dp', 'mlp'))
- input_grad: bfloat16 [2048, 8, 1024], P('head', ('dp', 'mlp'))
- first_values_grad: bfloat16 [2048, 8, 1024], P(None, ('dp', 'mlp'), 'head')
- attn_gain_grad: float32 [1024], replicated
- w_query_grad: float32 [1024, 1024], P(None, 'head')
- w_key_grad: float32 [1024, 1024], P(None, 'head')
- w_value_grad: float32 [1024, 1024], P(None, 'head')
- w_out_grad: float32 [1024, 1024], P('head')
- mlp_gain_grad: float32 [1024], replicated
- w_gate_grad: float32 [1024, 2816], P(None, 'mlp')
- w_up_grad: float32 [1024, 2816], P(None, 'mlp')
- w_down_grad: float32 [2816, 1024], P('mlp')
- value_norms: float32 [2], replicated
Inputs may be any that keep to these rules, and one draw needn't show every extreme that they name: `segment_ids`: along each packed row (dimension 0) the ids start at 0 and rise by at most one from one position to the next; packed row 0 holds a single document, every other packed row exactly 8. `positions`: 0 at a row's start and wherever the segment id changes, else one more than at the previous position.
All inputs are finite; a program needn't handle non-finite values.
Results may differ from a plain program's by a relative error of at most 0.019.
Values may be sent and summed in bfloat16 or wider, within the bound.
No kernel may reach another device: no remote copies, remote signals or barrier semaphores. Data moves between devices by JAX's collectives and lax.ppermute only.
A program may use at most 256 MiB of HBM per device.

v0:
```python
import jax
import jax.numpy as jnp
from jax import lax
from jax.sharding import PartitionSpec as P

HEAD_DIM = 64
epsilon = 1e-06
theta_base = 10000.0
blend_weight = 0.5
masked_score = -1e30


def rms_scale(rows):
    return lax.rsqrt(jnp.mean(rows * rows, axis=-1, keepdims=True) + epsilon)


def norm_back(rows, scale, gain, grad):
    weighted = grad * gain
    row_grad = scale * weighted - rows * scale * scale * scale * jnp.mean(
        weighted * rows, axis=-1, keepdims=True
    )
    gain_grad = jnp.sum(grad * rows * scale, axis=(0, 1))
    return (row_grad, gain_grad)


def rotate(values, places, direction):
    half = values.shape[-1] // 2
    freq = theta_base ** (-jnp.arange(half, dtype=jnp.float32) * 2.0 / values.shape[-1])
    angles = places.astype(jnp.float32)[..., None] * freq
    cosine = jnp.cos(angles)[:, :, None, :]
    sine = direction * jnp.sin(angles)[:, :, None, :]
    first, second = (values[..., :half], values[..., half:])
    return jnp.concatenate(
        [first * cosine - second * sine, second * cosine + first * sine], axis=-1
    )


def by_rows(array, heads):
    return jnp.moveaxis(array.reshape(array.shape[0], array.shape[1], heads, -1), 1, 0)


def block_scores(queries, keys, segments, number, block):
    length = keys.shape[0]
    begin = number * block
    query_block = lax.dynamic_slice_in_dim(queries, begin, block, 0)
    query_index = begin + jnp.arange(block, dtype=jnp.int32)
    key_index = jnp.arange(length, dtype=jnp.int32)
    query_segments = lax.dynamic_slice_in_dim(segments, begin, block, 0)
    allowed = (key_index[None, :] <= query_index[:, None]) & (
        segments[None, :] == query_segments[:, None]
    )
    scores = jnp.einsum(
        "qhd,khd->hqk", query_block, keys, preferred_element_type=jnp.float32
    ) * HEAD_DIM ** (-0.5)
    return (query_block, jnp.where(allowed[None], scores, masked_score))


def attend_forward(queries, keys, values, segments, block):
    length = queries.shape[0]

    def one_block(carry, number):
        query_block, scores = block_scores(queries, keys, segments, number, block)
        top = jnp.max(scores, axis=-1, keepdims=True)
        log_total = top + jnp.log(jnp.sum(jnp.exp(scores - top), axis=-1, keepdims=True))
        weights = jnp.exp(scores - log_total).astype(jnp.bfloat16)
        mixed = jnp.einsum("hqk,khd->qhd", weights, values, preferred_element_type=jnp.float32)
        return (carry, (mixed, log_total))

    _, (mixed, log_total) = lax.scan(one_block, 0, jnp.arange(length // block))
    return (mixed.reshape(length, mixed.shape[2], mixed.shape[3]), log_total)


def attend_backward(queries, keys, values, segments, mixed_grad, log_total, block):
    length = queries.shape[0]
    scale = HEAD_DIM ** (-0.5)

    def one_block(carry, number):
        key_grad, value_grad = carry
        query_block, scores = block_scores(queries, keys, segments, number, block)
        probs = jnp.exp(scores - log_total[number])
        weights = probs.astype(jnp.bfloat16)
        grad_block = lax.dynamic_slice_in_dim(mixed_grad, number * block, block, 0)
        weight_grad = jnp.einsum(
            "qhd,khd->hqk", grad_block, values, preferred_element_type=jnp.float32
        )
        score_grad = (
            probs * (weight_grad - jnp.sum(probs * weight_grad, axis=-1, keepdims=True))
        ).astype(jnp.bfloat16)
        query_grad = (
            jnp.einsum("hqk,khd->qhd", score_grad, keys, preferred_element_type=jnp.float32) * scale
        )
        key_grad = (
            key_grad
            + jnp.einsum(
                "hqk,qhd->khd", score_grad, query_block, preferred_element_type=jnp.float32
            )
            * scale
        )
        value_grad = value_grad + jnp.einsum(
            "hqk,qhd->khd", weights, grad_block, preferred_element_type=jnp.float32
        )
        return ((key_grad, value_grad), query_grad)

    zeros = jnp.zeros(keys.shape, jnp.float32)
    (key_grad, value_grad), query_grad = lax.scan(
        one_block, (zeros, zeros), jnp.arange(length // block)
    )
    return (query_grad.reshape(keys.shape), key_grad, value_grad)


def on_device(
    tokens,
    first_values,
    segment_ids,
    positions,
    attn_gain,
    w_query,
    w_key,
    w_value,
    w_out,
    mlp_gain,
    w_gate,
    w_up,
    w_down,
    out_grad,
):
    width = w_query.shape[1]
    heads_here = width // HEAD_DIM
    length = segment_ids.shape[0]
    rows_here = tokens.shape[1]
    block = min(512, length)
    ff_here = w_gate.shape[1]
    residual = tokens.astype(jnp.float32)
    attn_scale = rms_scale(residual)
    attn_input = (residual * attn_scale * attn_gain).astype(jnp.bfloat16)
    w_project = jnp.concatenate([w_query, w_key, w_value], axis=1)
    piece = lax.all_gather(attn_input, "head", axis=0, tiled=True)
    count = piece.shape[0]
    joined = jnp.einsum("lrd,dh->lrh", piece, w_project, preferred_element_type=jnp.float32)
    query_part = joined[..., :width].reshape(count, rows_here, heads_here, HEAD_DIM)
    key_part = joined[..., width : 2 * width].reshape(count, rows_here, heads_here, HEAD_DIM)
    queries = (
        rotate(query_part, positions, 1.0).reshape(count, rows_here, width).astype(jnp.bfloat16)
    )
    keys = rotate(key_part, positions, 1.0).reshape(count, rows_here, width).astype(jnp.bfloat16)
    gathered, queries, keys, value_proj = (piece, queries, keys, joined[..., 2 * width :])
    firsts = first_values.astype(jnp.float32)
    blended = blend_weight * value_proj + (1.0 - blend_weight) * firsts
    blended_low = blended.astype(jnp.bfloat16)
    first_heads = firsts.reshape(length, rows_here, heads_here, HEAD_DIM)
    blend_heads = blended.reshape(length, rows_here, heads_here, HEAD_DIM)
    norm_local = jnp.stack(
        [
            jnp.sum(jnp.sqrt(jnp.sum(first_heads * first_heads, axis=-1))),
            jnp.sum(jnp.sqrt(jnp.sum(blend_heads * blend_heads, axis=-1))),
        ]
    )
    segment_rows = jnp.transpose(segment_ids, (1, 0))
    query_rows = by_rows(queries, heads_here)
    key_rows = by_rows(keys, heads_here)
    value_rows = by_rows(blended_low, heads_here)

    def forward_row(item):
        return attend_forward(item[0], item[1], item[2], item[3], block)

    mixed, log_total = lax.map(forward_row, (query_rows, key_rows, value_rows, segment_rows))
    attn_mixed = jnp.moveaxis(mixed, 0, 1).reshape(length, rows_here, width).astype(jnp.bfloat16)
    part = attn_mixed
    attn_branch = lax.psum_scatter(
        jnp.einsum("lrh,hd->lrd", part, w_out, preferred_element_type=jnp.float32),
        "head",
        scatter_dimension=0,
        tiled=True,
    )
    hidden_state = residual + attn_branch
    mlp_scale = rms_scale(hidden_state)
    mlp_input = (hidden_state * mlp_scale * mlp_gain).astype(jnp.bfloat16)
    w_gate_up = jnp.concatenate([w_gate, w_up], axis=1)
    piece = lax.all_gather(mlp_input, "mlp", axis=1, tiled=True)
    joined = jnp.einsum("lrd,df->lrf", piece, w_gate_up, preferred_element_type=jnp.float32)
    gate = joined[..., :ff_here]
    up = joined[..., ff_here:]
    expand_hidden = (jax.nn.silu(gate) * up).astype(jnp.bfloat16)
    mlp_gathered = piece
    down_terms = jnp.einsum(
        "lrf,fd->lrd", expand_hidden, w_down, preferred_element_type=jnp.float32
    )
    mlp_branch = lax.psum_scatter(
        down_terms.astype(jnp.bfloat16), "mlp", scatter_dimension=1, tiled=True
    ).astype(jnp.float32)
    output = (hidden_state + mlp_branch).astype(jnp.bfloat16)
    piece = lax.all_gather(out_grad, "mlp", axis=1, tiled=True)
    down_sum = jnp.einsum("lrf,lrd->fd", expand_hidden, piece, preferred_element_type=jnp.float32)
    part_grad = jnp.einsum("lrd,fd->lrf", piece, w_down, preferred_element_type=jnp.float32)
    hidden_grad = part_grad
    gate, up = (gate, up)
    sigma = jax.nn.sigmoid(gate)
    gate_grad = (hidden_grad * up * sigma * (1.0 + gate * (1.0 - sigma))).astype(jnp.bfloat16)
    up_grad = (hidden_grad * gate * sigma).astype(jnp.bfloat16)
    gate_up_grad = jnp.concatenate([gate_grad, up_grad], axis=-1)
    gate_up_wgrad = jnp.einsum(
        "lrd,lrf->df", mlp_gathered, gate_up_grad, preferred_element_type=jnp.float32
    )
    input_terms = jnp.einsum(
        "lrf,df->lrd", gate_up_grad, w_gate_up, preferred_element_type=jnp.float32
    )
    mlp_normed_grad = lax.psum_scatter(
        input_terms.astype(jnp.bfloat16), "mlp", scatter_dimension=1, tiled=True
    ).astype(jnp.float32)
    state_norm_grad, mlp_gain_grad = norm_back(hidden_state, mlp_scale, mlp_gain, mlp_normed_grad)
    state_grad = out_grad.astype(jnp.float32) + state_norm_grad
    state_grad_low = state_grad.astype(jnp.bfloat16)
    piece = lax.all_gather(state_grad_low, "head", axis=0, tiled=True)
    out_sum = jnp.einsum("lrh,lrd->hd", attn_mixed, piece, preferred_element_type=jnp.float32)
    part_grad = jnp.einsum("lrd,hd->lrh", piece, w_out, preferred_element_type=jnp.float32)
    out_wgrad = out_sum
    mixed_grad_low = part_grad.astype(jnp.bfloat16)
    mixed_grad_rows = by_rows(mixed_grad_low, heads_here)

    def backward_row(item):
        return attend_backward(item[0], item[1], item[2], item[3], item[4], item[5], block)

    query_grad, key_grad, blend_grad = lax.map(
        backward_row, (query_rows, key_rows, value_rows, segment_rows, mixed_grad_rows, log_total)
    )
    query_grad = jnp.moveaxis(query_grad, 0, 1)
    key_grad = jnp.moveaxis(key_grad, 0, 1)
    blend_low = (
        jnp.moveaxis(blend_grad, 0, 1).reshape(length, rows_here, width).astype(jnp.bfloat16)
    )
    query_pre = (
        rotate(query_grad, positions, -1.0).reshape(length, rows_here, width).astype(jnp.bfloat16)
    )
    key_pre = (
        rotate(key_grad, positions, -1.0).reshape(length, rows_here, width).astype(jnp.bfloat16)
    )
    value_pre = (blend_weight * blend_low.astype(jnp.float32)).astype(jnp.bfloat16)
    first_values_grad = ((1.0 - blend_weight) * blend_low.astype(jnp.float32)).astype(jnp.bfloat16)
    proj_grad = jnp.concatenate([query_pre, key_pre, value_pre], axis=-1)
    proj_wgrad = jnp.einsum("lrd,lrh->dh", gathered, proj_grad, preferred_element_type=jnp.float32)
    part = proj_grad
    attn_normed_grad = lax.psum_scatter(
        jnp.einsum("lrh,dh->lrd", part, w_project, preferred_element_type=jnp.float32).astype(
            jnp.bfloat16
        ),
        "head",
        scatter_dimension=0,
        tiled=True,
    ).astype(jnp.float32)
    input_norm_grad, attn_gain_grad = norm_back(residual, attn_scale, attn_gain, attn_normed_grad)
    input_grad = (state_grad + input_norm_grad).astype(jnp.bfloat16)
    query_wgrad, key_wgrad, value_wgrad, out_wgrad = (
        lax.psum(proj_wgrad[:, :width].astype(jnp.bfloat16), ("dp", "mlp")).astype(jnp.float32),
        lax.psum(proj_wgrad[:, width : 2 * width].astype(jnp.bfloat16), ("dp", "mlp")).astype(
            jnp.float32
        ),
        lax.psum(proj_wgrad[:, 2 * width :].astype(jnp.bfloat16), ("dp", "mlp")).astype(
            jnp.float32
        ),
        lax.psum(out_wgrad.astype(jnp.bfloat16), ("dp", "mlp")).astype(jnp.float32),
    )
    gate_wgrad, up_wgrad, down_wgrad = (
        lax.psum(gate_up_wgrad[:, :ff_here].astype(jnp.bfloat16), ("dp", "head")).astype(
            jnp.float32
        ),
        lax.psum(gate_up_wgrad[:, ff_here:].astype(jnp.bfloat16), ("dp", "head")).astype(
            jnp.float32
        ),
        lax.psum(down_sum.astype(jnp.bfloat16), ("dp", "head")).astype(jnp.float32),
    )
    attn_gain_total, mlp_gain_total, norm_total = lax.psum(
        (attn_gain_grad, mlp_gain_grad, norm_local), ("dp", "head", "mlp")
    )
    count_all = (
        length
        * rows_here
        * heads_here
        * lax.axis_size("dp")
        * lax.axis_size("head")
        * lax.axis_size("mlp")
    )
    value_norms = norm_total / count_all
    return (
        output,
        input_grad,
        first_values_grad,
        attn_gain_total,
        query_wgrad,
        key_wgrad,
        value_wgrad,
        out_wgrad,
        mlp_gain_total,
        gate_wgrad,
        up_wgrad,
        down_wgrad,
        value_norms,
    )


def solution(mesh):
    placed = (
        P("head", ("dp", "mlp"), None),
        P(None, ("dp", "mlp"), "head"),
        P(None, ("dp", "mlp")),
        P(None, ("dp", "mlp")),
        P(),
        P(None, "head"),
        P(None, "head"),
        P(None, "head"),
        P("head", None),
        P(),
        P(None, "mlp"),
        P(None, "mlp"),
        P("mlp", None),
        P("head", ("dp", "mlp"), None),
    )
    return jax.shard_map(
        on_device,
        mesh=mesh,
        in_specs=placed,
        out_specs=(
            P("head", ("dp", "mlp"), None),
            P("head", ("dp", "mlp"), None),
            P(None, ("dp", "mlp"), "head"),
            P(),
            P(None, "head"),
            P(None, "head"),
            P(None, "head"),
            P("head", None),
            P(),
            P(None, "mlp"),
            P(None, "mlp"),
            P("mlp", None),
            P(),
        ),
        check_vma=False,
    )
```

profile of v0, /device:TPU:0, one launch (start us, length us, event | category | flops | bytes accessed | tf_op | source)
XLA Modules:
  0.0 1060.9 jit_solution(17914866796289467341)
XLA Ops:
  19.0 48.6 %all-gather.5.cloned.1.call-done = bf16[2048,1,1024]{2,0,1:T(8,128)(2,1)} async-done(((bf16[512,1,1024]{2,0,1:T(8,128)(2,1)}), bf16[2048,1,1024]{2,0,1:T(8,128)(2,1)}) %all-gather.5.cloned.1.call-update) | async-done | bytes 4194320 | tf_op jit(solution)/shard_map/all_gather | solution.py:137
  67.6 5.8 fusion.45
  73.4 3.7 fusion.84
  78.5 68.2 %while.47 = (s32[]{:T(128)}, bf16[4,512,4,64]{1,3,2,0:T(8,128)(2,1)}, f32[4,4,512,1]{2,1,3,0:T(4,128)}, s32[4]{0:T(128)S(1)}, s32[2048]{0:T(1024)S(1)}, /*index=...) while((s32[]{:T(128)}, ...), condition=%wide.region_4.0_spmd, body=%wide.region_1.4_spmd.sunk | while | flops 1123023360 | bytes 65882372 | solution.py:69
  84.2 4.3 exponential_reduce_fusion.2
  89.2 5.5 fusion.136
  101.2 4.3 exponential_reduce_fusion.2
  106.2 5.5 fusion.136
  118.2 4.3 exponential_reduce_fusion.2
  123.2 5.5 fusion.136
  135.2 4.3 exponential_reduce_fusion.2
  140.2 5.5 fusion.136
  150.4 4.6 convolution_bitcast_fusion
  155.0 86.5 %reduce-scatter.5.cloned.1.call-done = f32[512,1,1024]{2,0,1:T(8,128)} async-done(((f32[2048,1,1024]{2,0,1:T(8,128)}), f32[512,1,1024]{2,0,1:T(8,128)}) %reduce-scatter.5.cloned.1.call-update) | async-done | bytes 2097168 | tf_op jit(solution)/shard_map/reduce_scatter | solution.py:169
  253.5 75.0 %all-gather.7.cloned.1.call-done = bf16[512,4,1024]{2,0,1:T(8,128)(2,1)} async-done(((bf16[512,1,1024]{2,0,1:T(8,128)(2,1)}), bf16[512,4,1024]{2,0,1:T(8,128)(2,1)}) %all-gather.7.cloned.1.call-update) | async-done | bytes 4194320 | tf_op jit(solution)/shard_map/all_gather | solution.py:179
  328.5 13.2 %fusion.74 = f32[512,4,1408]{0,2,1:T(8,128)} fusion(bf16[512,4,1024]{2,0,1:T(8,128)(2,1)} %all-gather.7.cloned.1.call-done, bf16[1024,704]{1,0:T(8,128)(2,1)} %copy.69, bf16[1024,704]{1,0:T(8,128)(2,1)} %copy.68), kind=kOutput, calls=%fused_computation.106 | convolution fusion | flops 5911347200 | bytes 18612224 | tf_op jit(solution)/shard_map/lrd,df->lrf/dot_general | solution.py:180
  341.7 67.6 %all-gather.9.cloned.1.call-done = bf16[512,4,1024]{2,0,1:T(8,128)(2,1)} async-done(((bf16[512,1,1024]{2,0,1:T(8,128)(2,1)}), bf16[512,4,1024]{2,0,1:T(8,128)(2,1)}) %all-gather.9.cloned.1.call-update) | async-done | bytes 4194320 | tf_op jit(solution)/shard_map/all_gather | solution.py:192
  409.3 10.6 multiply_convert_fusion.2
  422.4 9.5 fusion.49
  432.4 75.0 %reduce-scatter.9.cloned.1.call-done = bf16[512,1,1024]{2,0,1:T(8,128)(2,1)} async-done(((bf16[512,4,1024]{2,0,1:T(8,128)(2,1)}), bf16[512,1,1024]{2,0,1:T(8,128)(2,1)}) %reduce-scatter.9.cloned.1.call-update) | async-done | bytes 1048592 | tf_op jit(solution)/shard_map/reduce_scatter | solution.py:207
  507.4 3.2 fusion.69
  511.2 3.3 fusion.91
  514.7 10.4 bitcast_convert_fusion
  528.4 4.3 bitcast_convert_fusion.1
  532.8 35.1 %all-gather.11.cloned.1.call-done = bf16[2048,1,1024]{2,0,1:T(8,128)(2,1)} async-done(((bf16[512,1,1024]{2,0,1:T(8,128)(2,1)}), bf16[2048,1,1024]{2,0,1:T(8,128)(2,1)}) %all-gather.11.cloned.1.call-update) | async-done | bytes 4194320 | tf_op jit(solution)/shard_map/all_gather | solution.py:213
  568.0 4.4 fusion.50
  572.4 260.4 %while.48 = (s32[]{:T(128)}, f32[2048,4,64]{0,2,1:T(8,128)}, f32[2048,4,64]{0,2,1:T(8,128)}, f32[4,512,4,64]{1,0,3,2:T(4,128)}, s32[4]{0:T(128)S(1)}, /*index=5*...) while((s32[]{:T(128)}, f32[2048,4,64]{0,2,1:T(8,128)}, ...), condition=%wide.region_12.13_spmd.clone, body=%wide.region_10.12_spmd.clone.sunk | while | flops 2753165824 | bytes 212412720 | solution.py:105
  577.2 3.4 fusion.146
  580.6 5.8 copy-done.1
  586.5 7.2 fusion.149
  593.6 13.0 %multiply_reduce_fusion.3 = (f32[4,512]{1,0:T(4,128)S(1)}, f32[4,512,2048]{2,1,0:T(8,128)}) fusion(f32[4,512,2048]{2,1,0:T(8,128)} %copy-done.1, f32[4,512]{1,0:T(4,128)S(1)} %dynamic-slice_bitcast_fusion.2, pred[512,2048]{1,0:T(8,128)(4,1)S(1)} %fusion.147, bf16[2048,4,64]{0,2,1:T(8,128)(2,1)} %get-tuple-element.557, ...), kind=kOutput, calls=%fused_computation.19.clone.1 | convolution fusion | flops 557840384 | bytes 35930116 | tf_op jit(solution)/shard_map/while/body/eval_jaxpr/while/body/eval_jaxpr/qhd,khd->hqk/dot_general | solution.py:83
  606.6 12.3 %multiply_convert_fusion.7 = bf16[4,512,2048]{2,1,0:T(8,128)(2,1)S(1)} fusion(f32[4,512,2048]{2,1,0:T(8,128)} %get-tuple-element.477, f32[4,512,2048]{2,1,0:T(8,128)} %copy-done.1, f32[4,512]{1,0:T(4,128)S(1)} %get-tuple-element.478, f32[4,512]{1,0:T(4,128)S(1)} %dynamic-slice_bitcast_fusion.2, pred[512,2048]{1,0:T(8,128)(4,1)S(1)} %fusion.147), kind=kLoop, calls=%fused_computation.18.clone.1 | loop fusion | flops 25165824 | bytes 43008000 | tf_op jit(solution)/shard_map/while/body/eval_jaxpr/while/body/eval_jaxpr/convert_element_type | solution.py:88
  621.5 4.0 fusion.148
  626.0 11.1 %dynamic_update_slice.31 = f32[4,512,4,64]{1,0,3,2:T(4,128)} dynamic-update-slice(f32[4,512,4,64]{1,0,3,2:T(4,128)} %get-tuple-element.534, f32[1,512,4,64]{1,0,3,2:T(1,128)S(1)} %copy.97, s32[]{:T(128)S(6)} %copy.116, s32[]{:T(128)} %constant.102.clone.1..sunk.1, s32[]{:T(128)} %constant.102.clone.1..sunk.1, s32[]{:T(128)} %constant.102.clone.1..sunk.1) | dynamic-update-slice | bytes 1048580 | tf_op jit(solution)/shard_map/while/body/eval_jaxpr/while/body/jit(dynamic_update_index_in_dim)/dynamic_update_slice | solution.py:69
  641.8 3.3 fusion.146
  645.1 5.9 copy-done.1
  651.0 7.6 fusion.149
  658.6 12.8 %multiply_reduce_fusion.3 = (f32[4,512]{1,0:T(4,128)S(1)}, f32[4,512,2048]{2,1,0:T(8,128)}) fusion(f32[4,512,2048]{2,1,0:T(8,128)} %copy-done.1, f32[4,512]{1,0:T(4,128)S(1)} %dynamic-slice_bitcast_fusion.2, pred[512,2048]{1,0:T(8,128)(4,1)S(1)} %fusion.147, bf16[2048,4,64]{0,2,1:T(8,128)(2,1)} %get-tuple-element.557, ...), kind=kOutput, calls=%fused_computation.19.clone.1 | convolution fusion | flops 557840384 | bytes 35930116 | tf_op jit(solution)/shard_map/while/body/eval_jaxpr/while/body/eval_jaxpr/qhd,khd->hqk/dot_general | solution.py:83
  671.4 12.1 %multiply_convert_fusion.7 = bf16[4,512,2048]{2,1,0:T(8,128)(2,1)S(1)} fusion(f32[4,512,2048]{2,1,0:T(8,128)} %get-tuple-element.477, f32[4,512,2048]{2,1,0:T(8,128)} %copy-done.1, f32[4,512]{1,0:T(4,128)S(1)} %get-tuple-element.478, f32[4,512]{1,0:T(4,128)S(1)} %dynamic-slice_bitcast_fusion.2, pred[512,2048]{1,0:T(8,128)(4,1)S(1)} %fusion.147), kind=kLoop, calls=%fused_computation.18.clone.1 | loop fusion | flops 25165824 | bytes 43008000 | tf_op jit(solution)/shard_map/while/body/eval_jaxpr/while/body/eval_jaxpr/convert_element_type | solution.py:88
  686.1 4.7 fusion.148
  691.3 11.1 %dynamic_update_slice.31 = f32[4,512,4,64]{1,0,3,2:T(4,128)} dynamic-update-slice(f32[4,512,4,64]{1,0,3,2:T(4,128)} %get-tuple-element.534, f32[1,512,4,64]{1,0,3,2:T(1,128)S(1)} %copy.97, s32[]{:T(128)S(6)} %copy.116, s32[]{:T(128)} %constant.102.clone.1..sunk.1, s32[]{:T(128)} %constant.102.clone.1..sunk.1, s32[]{:T(128)} %constant.102.clone.1..sunk.1) | dynamic-update-slice | bytes 1048580 | tf_op jit(solution)/shard_map/while/body/eval_jaxpr/while/body/jit(dynamic_update_index_in_dim)/dynamic_update_slice | solution.py:69
  707.0 3.3 fusion.146
  710.4 5.7 copy-done.1
  716.1 7.5 fusion.149
  723.7 12.8 %multiply_reduce_fusion.3 = (f32[4,512]{1,0:T(4,128)S(1)}, f32[4,512,2048]{2,1,0:T(8,128)}) fusion(f32[4,512,2048]{2,1,0:T(8,128)} %copy-done.1, f32[4,512]{1,0:T(4,128)S(1)} %dynamic-slice_bitcast_fusion.2, pred[512,2048]{1,0:T(8,128)(4,1)S(1)} %fusion.147, bf16[2048,4,64]{0,2,1:T(8,128)(2,1)} %get-tuple-element.557, ...), kind=kOutput, calls=%fused_computation.19.clone.1 | convolution fusion | flops 557840384 | bytes 35930116 | tf_op jit(solution)/shard_map/while/body/eval_jaxpr/while/body/eval_jaxpr/qhd,khd->hqk/dot_general | solution.py:83
  736.5 12.1 %multiply_convert_fusion.7 = bf16[4,512,2048]{2,1,0:T(8,128)(2,1)S(1)} fusion(f32[4,512,2048]{2,1,0:T(8,128)} %get-tuple-element.477, f32[4,512,2048]{2,1,0:T(8,128)} %copy-done.1, f32[4,512]{1,0:T(4,128)S(1)} %get-tuple-element.478, f32[4,512]{1,0:T(4,128)S(1)} %dynamic-slice_bitcast_fusion.2, pred[512,2048]{1,0:T(8,128)(4,1)S(1)} %fusion.147), kind=kLoop, calls=%fused_computation.18.clone.1 | loop fusion | flops 25165824 | bytes 43008000 | tf_op jit(solution)/shard_map/while/body/eval_jaxpr/while/body/eval_jaxpr/convert_element_type | solution.py:88
  751.2 4.7 fusion.148
  756.4 11.1 %dynamic_update_slice.31 = f32[4,512,4,64]{1,0,3,2:T(4,128)} dynamic-update-slice(f32[4,512,4,64]{1,0,3,2:T(4,128)} %get-tuple-element.534, f32[1,512,4,64]{1,0,3,2:T(1,128)S(1)} %copy.97, s32[]{:T(128)S(6)} %copy.116, s32[]{:T(128)} %constant.102.clone.1..sunk.1, s32[]{:T(128)} %constant.102.clone.1..sunk.1, s32[]{:T(128)} %constant.102.clone.1..sunk.1) | dynamic-update-slice | bytes 1048580 | tf_op jit(solution)/shard_map/while/body/eval_jaxpr/while/body/jit(dynamic_update_index_in_dim)/dynamic_update_slice | solution.py:69
  772.1 3.3 fusion.146
  775.5 5.7 copy-done.1
  781.2 7.6 fusion.149
  788.8 12.8 %multiply_reduce_fusion.3 = (f32[4,512]{1,0:T(4,128)S(1)}, f32[4,512,2048]{2,1,0:T(8,128)}) fusion(f32[4,512,2048]{2,1,0:T(8,128)} %copy-done.1, f32[4,512]{1,0:T(4,128)S(1)} %dynamic-slice_bitcast_fusion.2, pred[512,2048]{1,0:T(8,128)(4,1)S(1)} %fusion.147, bf16[2048,4,64]{0,2,1:T(8,128)(2,1)} %get-tuple-element.557, ...), kind=kOutput, calls=%fused_computation.19.clone.1 | convolution fusion | flops 557840384 | bytes 35930116 | tf_op jit(solution)/shard_map/while/body/eval_jaxpr/while/body/eval_jaxpr/qhd,khd->hqk/dot_general | solution.py:83
  801.6 12.1 %multiply_convert_fusion.7 = bf16[4,512,2048]{2,1,0:T(8,128)(2,1)S(1)} fusion(f32[4,512,2048]{2,1,0:T(8,128)} %get-tuple-element.477, f32[4,512,2048]{2,1,0:T(8,128)} %copy-done.1, f32[4,512]{1,0:T(4,128)S(1)} %get-tuple-element.478, f32[4,512]{1,0:T(4,128)S(1)} %dynamic-slice_bitcast_fusion.2, pred[512,2048]{1,0:T(8,128)(4,1)S(1)} %fusion.147), kind=kLoop, calls=%fused_computation.18.clone.1 | loop fusion | flops 25165824 | bytes 43008000 | tf_op jit(solution)/shard_map/while/body/eval_jaxpr/while/body/eval_jaxpr/convert_element_type | solution.py:88
  816.3 4.7 fusion.148
  821.5 11.1 %dynamic_update_slice.31 = f32[4,512,4,64]{1,0,3,2:T(4,128)} dynamic-update-slice(f32[4,512,4,64]{1,0,3,2:T(4,128)} %get-tuple-element.534, f32[1,512,4,64]{1,0,3,2:T(1,128)S(1)} %copy.97, s32[]{:T(128)S(6)} %copy.116, s32[]{:T(128)} %constant.102.clone.1..sunk.1, s32[]{:T(128)} %constant.102.clone.1..sunk.1, s32[]{:T(128)} %constant.102.clone.1..sunk.1) | dynamic-update-slice | bytes 1048580 | tf_op jit(solution)/shard_map/while/body/eval_jaxpr/while/body/jit(dynamic_update_index_in_dim)/dynamic_update_slice | solution.py:69
  841.2 3.5 fusion.75
  848.8 7.2 convert_bitcast_fusion
  856.0 7.2 convolution_convert_fusion
  876.4 3.4 convert_element_type.236
  881.1 33.1 %all-reduce.6.cloned.1.call-done = (bf16[1024,256]{1,0:T(8,128)(2,1)}, bf16[1024,256]{1,0:T(8,128)(2,1)}, bf16[1024,256]{1,0:T(8,128)(2,1)}, bf16[256,1024]{1,0:T(8,128)(2,1)}) async-done(((bf16[1024,256]{1,0:T(8,128)(2,1)}, bf16[1024,256]{1,0:T(8,128)(2,1)}, bf16[1024,256]{1,0:T(8,128)(2,1)}, bf16[256,1024]{1,0:T(8,128)(2,1)}), (bf16[1024,256]{1,0:T(8,128)(2,1)}, bf16[1024,256]{1,0:T(8,128)(2,1)}, ...) | async-done | bytes 2097168 | tf_op jit(solution)/shard_map/psum | solution.py:253
  920.7 48.6 %reduce-scatter.11.cloned.1.call-done = bf16[512,1,1024]{2,0,1:T(8,128)(2,1)} async-done(((bf16[2048,1,1024]{2,0,1:T(8,128)(2,1)}), bf16[512,1,1024]{2,0,1:T(8,128)(2,1)}) %reduce-scatter.11.cloned.1.call-update) | async-done | bytes 1048592 | tf_op jit(solution)/shard_map/reduce_scatter | solution.py:242
  972.0 42.0 %all-reduce = (f32[1024]{0:T(1024)}, f32[1024]{0:T(1024)}, f32[2]{0:T(128)}) all-reduce(f32[1024]{0:T(1024)} %get-tuple-element.261, f32[1024]{0:T(1024)} %get-tuple-element.259, f32[2]{0:T(128)} %pad_maximum_fusion.7), channel_id=1, replica_groups=mesh['dp'=2,'head'=4,'mlp'=4] {'dp','head','mlp'}, use_global_device_ids=true, to_apply=%region_16.17 | all-reduce | flops 2050 | bytes 16400 | tf_op jit(solution)/shard_map/psum | solution.py:271
  1016.5 32.9 %reduce-scatter.7.cloned.1.call-done = bf16[512,1,1024]{2,0,1:T(8,128)(2,1)} async-done(((bf16[512,4,1024]{2,0,1:T(8,128)(2,1)}), bf16[512,1,1024]{2,0,1:T(8,128)(2,1)}) %reduce-scatter.7.cloned.1.call-update) | async-done | bytes 1048592 | tf_op jit(solution)/shard_map/reduce_scatter | solution.py:188
  1049.4 4.4 fusion.63
  (223 shorter events, 122.3 us)
Async XLA Ops:
  7.2 402.2 %copy-start = (bf16[704,1024]{1,0:T(8,128)(2,1)S(1)}, bf16[704,1024]{1,0:T(8,128)(2,1)}, u32[]{:S(2)}) copy-start(bf16[704,1024]{1,0:T(8,128)(2,1)} %param.30) | copy-start | bytes 4325380
  7.2 4.9 copy-start.36
  7.2 4.9 copy-start.19
  7.2 60.4 %all-gather.5.cloned.1.call-start = ((), (), s32[]{:S(2)}) async-start(), calls=%async_computation.4 | async-start | bytes 5242880 | tf_op jit(solution)/shard_map/all_gather | solution.py:137
  8.9 0.6 copy-start.33
  12.0 229.5 %reduce-scatter.5.cloned.1.call-start = ((), (), s32[]{:S(2)}) async-start(), calls=%async_computation.5 | async-start | bytes 10485760 | tf_op jit(solution)/shard_map/reduce_scatter | solution.py:169
  16.1 1.2 copy-start.27
  19.0 58.1 %copy-start.13 = (f32[2048,32]{0,1:T(8,128)}, f32[2048,32]{0,1:T(8,128)S(1)}, u32[]{:S(2)}) copy-start(f32[2048,32]{0,1:T(8,128)S(1)} %get-tuple-element.348) | copy-start | bytes 786436
  77.8 0.7 copy-start.18
  84.2 5.0 copy-start.20
  94.7 1.0 copy-start.21
  101.2 5.0 copy-start.20
  111.7 1.0 copy-start.21
  118.2 5.0 copy-start.20
  128.7 1.0 copy-start.21
  135.2 5.0 copy-start.20
  145.7 1.0 copy-start.21
  146.7 8.3 copy-start.4
  146.7 3.7 copy-start.23
  149.4 1.0 copy-start.9
  154.9 86.6 %copy-start.2 = (bf16[512,1,1024]{2,0,1:T(8,128)(2,1)S(1)}, bf16[512,1,1024]{2,0,1:T(8,128)(2,1)}, u32[]{:S(2)}) copy-start(bf16[512,1,1024]{2,0,1:T(8,128)(2,1)} %param.18) | copy-start | bytes 3145732
  155.0 89.8 %copy-start.28 = (f32[1024]{0:T(1024)S(1)}, f32[1024]{0:T(1024)}, u32[]{:S(2)}) copy-start(f32[1024]{0:T(1024)} %param.27) | copy-start | bytes 12292
  155.0 173.5 %all-gather.7.cloned.1.call-start = ((), (), s32[]{:S(2)}) async-start(), calls=%async_computation.6 | async-start | bytes 5242880 | tf_op jit(solution)/shard_map/all_gather | solution.py:179
  244.8 265.9 %copy-start.30 = (f32[512]{0:T(512)}, f32[512]{0:T(512)S(1)}, u32[]{:S(2)}) copy-start(f32[512]{0:T(512)S(1)} %add_rsqrt_fusion) | copy-start | bytes 6148
  247.6 161.7 %all-gather.9.cloned.1.call-start = ((), (), s32[]{:S(2)}) async-start(), calls=%async_computation.8 | async-start | bytes 5242880 | tf_op jit(solution)/shard_map/all_gather | solution.py:192
  248.2 259.2 %reduce-scatter.9.cloned.1.call-start = ((), (), s32[]{:S(2)}) async-start(), calls=%async_computation.9 | async-start | bytes 5242880 | tf_op jit(solution)/shard_map/reduce_scatter | solution.py:207
  409.3 13.1 %copy-start.16 = (bf16[1024,704]{1,0:T(8,128)(2,1)S(1)}, bf16[1024,704]{1,0:T(8,128)(2,1)}, u32[]{:S(2)}) copy-start(bf16[1024,704]{1,0:T(8,128)(2,1)} %copy.68) | copy-start | bytes 4325380
  409.3 13.1 %copy-start.17 = (bf16[1024,704]{1,0:T(8,128)(2,1)S(1)}, bf16[1024,704]{1,0:T(8,128)(2,1)}, u32[]{:S(2)}) copy-start(bf16[1024,704]{1,0:T(8,128)(2,1)} %copy.69) | copy-start | bytes 4325380
  419.9 1.6 copy-start.41
  419.9 2.5 copy-start.42
  431.9 79.3 %copy-start.5 = (bf16[512,1,1024]{2,0,1:T(8,128)(2,1)S(1)}, bf16[512,1,1024]{2,0,1:T(8,128)(2,1)}, u32[]{:S(2)}) copy-start(bf16[512,1,1024]{2,0,1:T(8,128)(2,1)} %param.31) | copy-start | bytes 3145732
  431.9 136.0 %all-gather.11.cloned.1.call-start = ((), (), s32[]{:S(2)}) async-start(), calls=%async_computation.10 | async-start | bytes 5242880 | tf_op jit(solution)/shard_map/all_gather | solution.py:213
  507.4 3.9 copy-start.7
  510.6 0.6 copy-start.35
  514.6 356.7 %all-reduce.8.cloned.1.call-start = ((), (), s32[]{:S(2)}) async-start(), calls=%async_computation.13 | async-start | bytes 9175040 | tf_op jit(solution)/shard_map/psum | solution.py:263
  514.7 12.8 %copy-start.40 = (bf16[512,4,704]{0,2,1:T(8,128)(2,1)S(1)}, bf16[512,4,704]{0,2,1:T(8,128)(2,1)}, u32[]{:S(2)}) copy-start(bf16[512,4,704]{0,2,1:T(8,128)(2,1)} %get-tuple-element.321) | copy-start | bytes 8650756
  525.1 3.3 copy-start.39
  532.8 35.2 %copy-start.24 = (bf16[256,1024]{1,0:T(8,128)(2,1)S(1)}, bf16[256,1024]{1,0:T(8,128)(2,1)}, u32[]{:S(2)}) copy-start(bf16[256,1024]{1,0:T(8,128)(2,1)} %param.26) | copy-start | bytes 1572868
  532.8 381.4 %all-reduce.6.cloned.1.call-start = ((), (), s32[]{:S(2)}) async-start(), calls=%async_computation.12 | async-start | bytes 4194304 | tf_op jit(solution)/shard_map/psum | solution.py:253
  580.6 5.9 copy-start.1
  645.1 5.9 copy-start.1
  710.4 5.8 copy-start.1
  775.5 5.8 copy-start.1
  837.8 2.0 copy-start.14
  837.9 3.3 copy-start.37
  838.1 6.7 copy-start.22
  840.0 8.8 copy-start.11
  841.2 4.7 copy-start.38
  844.8 1.8 copy-start.10
  848.7 120.6 %reduce-scatter.11.cloned.1.call-start = ((), (), s32[]{:S(2)}) async-start(), calls=%async_computation.11 | async-start | bytes 5242880 | tf_op jit(solution)/shard_map/reduce_scatter | solution.py:242
  856.0 193.4 %reduce-scatter.7.cloned.1.call-start = ((), (), s32[]{:S(2)}) async-start(), calls=%async_computation.7 | async-start | bytes 5242880 | tf_op jit(solution)/shard_map/reduce_scatter | solution.py:188
  863.3 2.6 copy-start.8
  871.3 3.1 copy-start.15
  876.4 3.4 copy-start.12
  914.2 4.3 copy-start.26
  914.2 5.4 copy-start.25
  914.2 55.1 %copy-start.3 = (bf16[512,1,1024]{2,0,1:T(8,128)(2,1)S(1)}, bf16[512,1,1024]{2,0,1:T(8,128)(2,1)}, u32[]{:S(2)}) copy-start(bf16[512,1,1024]{2,0,1:T(8,128)(2,1)} %param.18) | copy-start | bytes 3145732
  914.2 55.1 %copy-start.32 = (f32[1024]{0:T(1024)S(1)}, f32[1024]{0:T(1024)}, u32[]{:S(2)}) copy-start(f32[1024]{0:T(1024)} %param.22) | copy-start | bytes 12292
  914.2 55.1 %copy-start.34 = (f32[512]{0:T(512)S(1)}, f32[512]{0:T(512)}, u32[]{:S(2)}) copy-start(f32[512]{0:T(512)} %copy-done.33) | copy-start | bytes 6148
  918.5 130.9 %copy-start.6 = (bf16[512,1,1024]{2,0,1:T(8,128)(2,1)S(1)}, bf16[512,1,1024]{2,0,1:T(8,128)(2,1)}, u32[]{:S(2)}) copy-start(bf16[512,1,1024]{2,0,1:T(8,128)(2,1)} %param.31) | copy-start | bytes 3145732
  918.5 130.9 %copy-start.29 = (f32[1024]{0:T(1024)S(1)}, f32[1024]{0:T(1024)}, u32[]{:S(2)}) copy-start(f32[1024]{0:T(1024)} %param.27) | copy-start | bytes 12292
  918.5 130.9 %copy-start.31 = (f32[512]{0:T(512)S(1)}, f32[512]{0:T(512)}, u32[]{:S(2)}) copy-start(f32[512]{0:T(512)} %copy-done.30) | copy-start | bytes 6148
Sparse Core Ops, SparseCore 0:
  12.2 55.3 all-gather.4
  155.1 86.4 reduce-scatter.4
  247.7 80.7 all-gather.6
  330.0 79.2 all-gather.8
  432.0 75.2 reduce-scatter.8
  514.7 53.1 all-gather.10
  572.2 85.7 all-reduce.7
  848.8 65.3 all-reduce.5
  917.2 52.1 reduce-scatter.10
  971.6 77.7 reduce-scatter.6
where the time goes:
time: 1070 us; the launch traced here: 1060 us
  waiting for transfers between devices  503 us (47%)
  matrix products  241 us (23%)
  other arithmetic  130 us (12%)
  local copies, waits for them, and re-layouts  117 us (11%)
  blocking collectives  42 us (4%)
  between operations  14.8 us (1%)
  loops' own time  12.4 us (1%)
    reduce_scatter x1, waiting for transfers between devices, on_device(): lax.psum_scatter(jnp.einsum('lrh,hd->lrd', part, w_out, preferred_element...  86.5 us
    reduce_scatter x1, waiting for transfers between devices, on_device(): lax.psum_scatter(input_terms.astype(jnp.bfloat16), 'mlp', scatter_dimensi...  75 us
    all_gather x1, waiting for transfers between devices, on_device(): piece = lax.all_gather(mlp_input, 'mlp', axis=1, tiled=True)  75 us
    all_gather x1, waiting for transfers between devices, on_device(): piece = lax.all_gather(out_grad, 'mlp', axis=1, tiled=True)  67.6 us
    dot_general x4, matrix products, one_block(): jnp.einsum('qhd,khd->hqk', grad_block, values, preferred_element_type=jnp...  51.3 us
    reduce_scatter x1, waiting for transfers between devices, on_device(): lax.psum_scatter(jnp.einsum('lrh,dh->lrd', part, w_project, preferred_ele...  48.6 us
    all_gather x1, waiting for transfers between devices, on_device(): piece = lax.all_gather(attn_input, 'head', axis=0, tiled=True)  48.6 us
    convert_element_type x4, other arithmetic, one_block(): score_grad = (probs * (weight_grad - jnp.sum(probs * weight_grad, axis=-1...  48.5 us
  transfers between devices with their start and end apart: 10, of which 9 were waited for; matrix products, arithmetic and copies ran while one was open for 31% of the time, Pallas kernels for 0%

commit v1 on v0

--- a/solution.py
+++ b/solution.py
@@ -176,7 +176,12 @@
     mlp_scale = rms_scale(hidden_state)
     mlp_input = (hidden_state * mlp_scale * mlp_gain).astype(jnp.bfloat16)
     w_gate_up = jnp.concatenate([w_gate, w_up], axis=1)
-    piece = lax.all_gather(mlp_input, "mlp", axis=1, tiled=True)
+    ring = [mlp_input]
+    for hop in range(3):
+        ring.append(lax.ppermute(ring[-1], "mlp", [(dev, (dev + 1) % 4) for dev in range(4)]))
+    piece = jnp.roll(
+        jnp.concatenate(ring[::-1], axis=1), (lax.axis_index("mlp") + 1) * ring[0].shape[1], axis=1
+    )
     joined = jnp.einsum("lrd,df->lrf", piece, w_gate_up, preferred_element_type=jnp.float32)
     gate = joined[..., :ff_here]
     up = joined[..., ff_here:]

time: 1070 us -> 950 us (0.89)
  waiting for transfers between devices: 503 us -> 369 us
    all_gather x1 -> x0, waiting for transfers between devices: 75 us -> none  [on_device(): piece = lax.all_gather(mlp_input, 'mlp', axis=1, tiled=True)]
    ppermute x0 -> x3, waiting for transfers between devices: none -> 70.7 us  [on_device(): lax.ppermute(ring[-1], 'mlp', [(dev, (dev + 1) % 4) for dev in range(4)])]
    all_gather x1, waiting for transfers between devices: 67.6 us -> 0.01 us  [on_device(): piece = lax.all_gather(out_grad, 'mlp', axis=1, tiled=True)]
    reduce_scatter x1, waiting for transfers between devices: 48.6 us -> 0.01 us  [on_device(): lax.psum_scatter(jnp.einsum('lrh,dh->lrd', part, w_project, preferred_ele...]
    reduce_scatter x1, waiting for transfers between devices: 32.9 us -> 17.4 us  [on_device(): lax.psum_scatter(down_terms.astype(jnp.bfloat16), 'mlp', scatter_dimensio...]
    unnamed x89 -> x101, local copies, waits for them, and re-layouts: 25.6 us -> 34.4 us
  transfers between devices with their start and end apart: 10 -> 12, of which waited for: 9 -> 9; matrix products, arithmetic and copies ran while one was open for 31% -> 36% of each run, Pallas kernels for 0% -> 0%
where the time goes in v1:
time: 950 us; the launch traced here: 943 us
  waiting for transfers between devices  369 us (39%)
  matrix products  238 us (25%)
  other arithmetic  133 us (14%)
  local copies, waits for them, and re-layouts  126 us (13%)
  blocking collectives  45.2 us (5%)
  between operations  16.2 us (2%)
  loops' own time  12.9 us (1%)
    reduce_scatter x1, waiting for transfers between devices, on_device(): lax.psum_scatter(jnp.einsum('lrh,hd->lrd', part, w_out, preferred_element...  85.9 us
    reduce_scatter x1, waiting for transfers between devices, on_device(): lax.psum_scatter(input_terms.astype(jnp.bfloat16), 'mlp', scatter_dimensi...  73.9 us
    ppermute x3, waiting for transfers between devices, on_device(): lax.ppermute(ring[-1], 'mlp', [(dev, (dev + 1) % 4) for dev in range(4)])  70.7 us
    dot_general x4, matrix products, one_block(): jnp.einsum('qhd,khd->hqk', grad_block, values, preferred_element_type=jnp...  51.3 us
    all_gather x1, waiting for transfers between devices, on_device(): piece = lax.all_gather(attn_input, 'head', axis=0, tiled=True)  48.6 us
    convert_element_type x4, other arithmetic, one_block(): score_grad = (probs * (weight_grad - jnp.sum(probs * weight_grad, axis=-1...  48.5 us
    dynamic_update_slice x8, local copies, waits for them, and re-layouts, attend_forward(): _, (mixed, log_total) = lax.scan(one_block, 0, jnp.arange(length // block))  46.6 us
    psum x1, blocking collectives, on_device(): lax.psum((attn_gain_grad, mlp_gain_grad, norm_local), ('dp', 'head', 'mlp'))  45.2 us
  transfers between devices with their start and end apart: 12, of which 9 were waited for; matrix products, arithmetic and copies ran while one was open for 36% of the time, Pallas kernels for 0%

profile of v1, /device:TPU:0, one launch (start us, length us, event | category | flops | bytes accessed | tf_op | source)
XLA Modules:
  0.0 942.9 jit_solution(6140633532916375657)
XLA Ops:
  19.8 48.6 %all-gather.4.cloned.1.call-done = bf16[2048,1,1024]{2,0,1:T(8,128)(2,1)} async-done(((bf16[512,1,1024]{2,0,1:T(8,128)(2,1)}), bf16[2048,1,1024]{2,0,1:T(8,128)(2,1)}) %all-gather.4.cloned.1.call-update) | async-done | bytes 4194320 | tf_op jit(solution)/shard_map/all_gather | solution.py:137
  68.4 5.8 fusion.45
  74.3 3.7 fusion.86
  79.3 68.3 %while.47 = (s32[]{:T(128)}, bf16[4,512,4,64]{1,3,2,0:T(8,128)(2,1)}, f32[4,4,512,1]{2,1,3,0:T(4,128)}, s32[4]{0:T(128)S(1)}, s32[2048]{0:T(1024)S(1)}, /*index=...) while((s32[]{:T(128)}, ...), condition=%wide.region_4.0_spmd, body=%wide.region_1.4_spmd.sunk | while | flops 1123023360 | bytes 65882372 | solution.py:69
  85.2 4.3 exponential_reduce_fusion.2
  90.1 5.5 fusion.138
  102.2 4.3 exponential_reduce_fusion.2
  107.1 5.5 fusion.138
  119.2 4.3 exponential_reduce_fusion.2
  124.1 5.5 fusion.138
  136.2 4.3 exponential_reduce_fusion.2
  141.2 5.5 fusion.138
  151.3 4.6 convolution_bitcast_fusion
  156.6 85.9 %reduce-scatter.5.cloned.1.call-done = f32[512,1,1024]{2,0,1:T(8,128)} async-done(((f32[2048,1,1024]{2,0,1:T(8,128)}), f32[512,1,1024]{2,0,1:T(8,128)}) %reduce-scatter.5.cloned.1.call-update) | async-done | bytes 2097168 | tf_op jit(solution)/shard_map/reduce_scatter | solution.py:169
  249.1 25.2 %collective-permute-done = bf16[512,1,1024]{2,0,1:T(8,128)(2,1)S(1)} collective-permute-done((bf16[512,1,1024]{2,0,1:T(8,128)(2,1)S(1)}, bf16[512,1,1024]{2,0,1:T(8,128)(2,1)S(1)}, u32[]{:S(2)}, u32[]{:S(2)}) %collective-permute-start) | collective-permute-done | bytes 1048608 | tf_op jit(solution)/shard_map/ppermute | solution.py:181
  274.3 25.9 %collective-permute-done.1 = bf16[512,1,1024]{2,0,1:T(8,128)(2,1)} collective-permute-done((bf16[512,1,1024]{2,0,1:T(8,128)(2,1)S(1)}, bf16[512,1,1024]{2,0,1:T(8,128)(2,1)}, u32[]{:S(2)}, u32[]{:S(2)}) %collective-permute-start.1) | collective-permute-done | bytes 1048608 | tf_op jit(solution)/shard_map/ppermute | solution.py:181
  305.8 19.6 %collective-permute-done.2 = bf16[512,1,1024]{2,0,1:T(8,128)(2,1)} collective-permute-done((bf16[512,1,1024]{2,0,1:T(8,128)(2,1)}, bf16[512,1,1024]{2,0,1:T(8,128)(2,1)}, u32[]{:S(2)}, u32[]{:S(2)}) %collective-permute-start.2) | collective-permute-done | bytes 1048608 | tf_op jit(solution)/shard_map/ppermute | solution.py:181
  337.8 10.7 %fusion.50 = f32[512,4,1408]{0,2,1:T(8,128)} fusion(bf16[512,8,1024]{2,0,1:T(8,128)(2,1)S(1)} %constant_dynamic-update-slice_fusion.3, s32[]{:T(128)S(6)} %select_n.33, bf16[1024,704]{1,0:T(8,128)(2,1)S(1)} %copy-done.18, bf16[1024,704]{1,0:T(8,128)(2,1)S(1)} %copy-done.16), kind=kOutput, calls=%fused_computation.71 | convolution fusion | flops 5911347200 | bytes 18874372 | tf_op jit(solution)/shard_map/lrd,df->lrf/dot_general | solution.py:185
  348.5 10.6 %multiply_convert_fusion.2 = (bf16[512,4,704]{0,2,1:T(8,128)(2,1)S(1)}, bf16[512,4,704]{0,2,1:T(8,128)(2,1)S(1)}, bf16[512,4,704]{0,2,1:T(8,128)(2,1)}) fusion(f32[512,4,1408]{0,2,1:T(8,128)} %fusion.50, bf16[512,4,1024]{2,0,1:T(8,128)(2,1)} %all-gather.6.cloned.1.call-done, bf16[704,1024]{1,0:T(8,128)(2,1)S(1)} %copy-done), kind=kOutput, calls=%fused_computation.50 | convolution fusion | flops 2975858688 | bytes 25821184 | tf_op jit(solution)/shard_map/lrd,fd->lrf/dot_general | solution.py:199
  361.6 9.4 %fusion.52 = bf16[512,4,1024]{2,0,1:T(8,128)(2,1)} fusion(bf16[512,4,704]{0,2,1:T(8,128)(2,1)S(1)} %get-tuple-element.320, bf16[512,4,704]{0,2,1:T(8,128)(2,1)S(1)} %get-tuple-element.319, bf16[1024,704]{1,0:T(8,128)(2,1)S(1)} %copy-done.19, bf16[1024,704]{1,0:T(8,128)(2,1)S(1)} %copy-done.17), kind=kOutput, calls=%fused_computation.76 | convolution fusion | flops 5924978688 | bytes 12845056 | tf_op jit(solution)/shard_map/lrf,df->lrd/dot_general | solution.py:209
  371.3 73.9 %reduce-scatter.9.cloned.1.call-done = bf16[512,1,1024]{2,0,1:T(8,128)(2,1)} async-done(((bf16[512,4,1024]{2,0,1:T(8,128)(2,1)}), bf16[512,1,1024]{2,0,1:T(8,128)(2,1)}) %reduce-scatter.9.cloned.1.call-update) | async-done | bytes 1048592 | tf_op jit(solution)/shard_map/reduce_scatter | solution.py:212
  445.2 3.2 fusion.72
  449.0 3.3 fusion.95
  452.5 10.4 %bitcast_convert_fusion = bf16[1024,1408]{1,0:T(8,128)(2,1)S(1)} fusion(bf16[512,4,704]{0,2,1:T(8,128)(2,1)} %copy-done.45, bf16[512,4,704]{0,2,1:T(8,128)(2,1)} %copy-done.44, bf16[512,8,1024]{2,0,1:T(8,128)(2,1)} %copy-done.32, s32[]{:T(128)S(6)} %select_n.33), kind=kOutput, calls=%fused_computation.48 | convolution fusion | flops 5918556160 | bytes 12845060 | tf_op jit(solution)/shard_map/lrd,lrf->df/dot_general | solution.py:206
  466.3 4.2 bitcast_convert_fusion.1
  470.6 37.3 %all-gather.8.cloned.1.call-done = bf16[2048,1,1024]{2,0,1:T(8,128)(2,1)} async-done(((bf16[512,1,1024]{2,0,1:T(8,128)(2,1)}), bf16[2048,1,1024]{2,0,1:T(8,128)(2,1)}) %all-gather.8.cloned.1.call-update) | async-done | bytes 4194320 | tf_op jit(solution)/shard_map/all_gather | solution.py:218
  507.9 4.4 fusion.53
  512.3 260.6 %while.48 = (s32[]{:T(128)}, f32[2048,4,64]{0,2,1:T(8,128)}, f32[2048,4,64]{0,2,1:T(8,128)}, f32[4,512,4,64]{1,0,3,2:T(4,128)}, s32[4]{0:T(128)S(1)}, /*index=5*...) while((s32[]{:T(128)}, f32[2048,4,64]{0,2,1:T(8,128)}, ...), condition=%wide.region_12.13_spmd.clone, body=%wide.region_10.12_spmd.clone.sunk | while | flops 2753165824 | bytes 212412720 | solution.py:105
  517.2 3.3 fusion.148
  520.5 5.9 copy-done.1
  526.4 7.2 fusion.151
  533.6 12.9 %multiply_reduce_fusion.3 = (f32[4,512]{1,0:T(4,128)S(1)}, f32[4,512,2048]{2,1,0:T(8,128)}) fusion(f32[4,512,2048]{2,1,0:T(8,128)} %copy-done.1, f32[4,512]{1,0:T(4,128)S(1)} %dynamic-slice_bitcast_fusion.2, pred[512,2048]{1,0:T(8,128)(4,1)S(1)} %fusion.149, bf16[2048,4,64]{0,2,1:T(8,128)(2,1)} %get-tuple-element.557, ...), kind=kOutput, calls=%fused_computation.19.clone.1 | convolution fusion | flops 557840384 | bytes 35930116 | tf_op jit(solution)/shard_map/while/body/eval_jaxpr/while/body/eval_jaxpr/qhd,khd->hqk/dot_general | solution.py:83
  546.5 12.3 %multiply_convert_fusion.7 = bf16[4,512,2048]{2,1,0:T(8,128)(2,1)S(1)} fusion(f32[4,512,2048]{2,1,0:T(8,128)} %get-tuple-element.477, f32[4,512,2048]{2,1,0:T(8,128)} %copy-done.1, f32[4,512]{1,0:T(4,128)S(1)} %get-tuple-element.478, f32[4,512]{1,0:T(4,128)S(1)} %dynamic-slice_bitcast_fusion.2, pred[512,2048]{1,0:T(8,128)(4,1)S(1)} %fusion.149), kind=kLoop, calls=%fused_computation.18.clone.1 | loop fusion | flops 25165824 | bytes 43008000 | tf_op jit(solution)/shard_map/while/body/eval_jaxpr/while/body/eval_jaxpr/convert_element_type | solution.py:88
  561.4 3.9 fusion.150
  565.9 11.1 %dynamic_update_slice.31 = f32[4,512,4,64]{1,0,3,2:T(4,128)} dynamic-update-slice(f32[4,512,4,64]{1,0,3,2:T(4,128)} %get-tuple-element.534, f32[1,512,4,64]{1,0,3,2:T(1,128)S(1)} %copy.97, s32[]{:T(128)S(6)} %copy.123, s32[]{:T(128)} %constant.124.clone.1..sunk.1, s32[]{:T(128)} %constant.124.clone.1..sunk.1, s32[]{:T(128)} %constant.124.clone.1..sunk.1) | dynamic-update-slice | bytes 1048580 | tf_op jit(solution)/shard_map/while/body/eval_jaxpr/while/body/jit(dynamic_update_index_in_dim)/dynamic_update_slice | solution.py:69
  581.7 3.3 fusion.148
  585.0 5.7 copy-done.1
  590.8 7.6 fusion.151
  598.3 12.8 %multiply_reduce_fusion.3 = (f32[4,512]{1,0:T(4,128)S(1)}, f32[4,512,2048]{2,1,0:T(8,128)}) fusion(f32[4,512,2048]{2,1,0:T(8,128)} %copy-done.1, f32[4,512]{1,0:T(4,128)S(1)} %dynamic-slice_bitcast_fusion.2, pred[512,2048]{1,0:T(8,128)(4,1)S(1)} %fusion.149, bf16[2048,4,64]{0,2,1:T(8,128)(2,1)} %get-tuple-element.557, ...), kind=kOutput, calls=%fused_computation.19.clone.1 | convolution fusion | flops 557840384 | bytes 35930116 | tf_op jit(solution)/shard_map/while/body/eval_jaxpr/while/body/eval_jaxpr/qhd,khd->hqk/dot_general | solution.py:83
  611.2 12.1 %multiply_convert_fusion.7 = bf16[4,512,2048]{2,1,0:T(8,128)(2,1)S(1)} fusion(f32[4,512,2048]{2,1,0:T(8,128)} %get-tuple-element.477, f32[4,512,2048]{2,1,0:T(8,128)} %copy-done.1, f32[4,512]{1,0:T(4,128)S(1)} %get-tuple-element.478, f32[4,512]{1,0:T(4,128)S(1)} %dynamic-slice_bitcast_fusion.2, pred[512,2048]{1,0:T(8,128)(4,1)S(1)} %fusion.149), kind=kLoop, calls=%fused_computation.18.clone.1 | loop fusion | flops 25165824 | bytes 43008000 | tf_op jit(solution)/shard_map/while/body/eval_jaxpr/while/body/eval_jaxpr/convert_element_type | solution.py:88
  625.9 4.7 fusion.150
  631.1 11.1 %dynamic_update_slice.31 = f32[4,512,4,64]{1,0,3,2:T(4,128)} dynamic-update-slice(f32[4,512,4,64]{1,0,3,2:T(4,128)} %get-tuple-element.534, f32[1,512,4,64]{1,0,3,2:T(1,128)S(1)} %copy.97, s32[]{:T(128)S(6)} %copy.123, s32[]{:T(128)} %constant.124.clone.1..sunk.1, s32[]{:T(128)} %constant.124.clone.1..sunk.1, s32[]{:T(128)} %constant.124.clone.1..sunk.1) | dynamic-update-slice | bytes 1048580 | tf_op jit(solution)/shard_map/while/body/eval_jaxpr/while/body/jit(dynamic_update_index_in_dim)/dynamic_update_slice | solution.py:69
  646.9 3.3 fusion.148
  650.2 5.7 copy-done.1
  656.0 7.5 fusion.151
  663.5 12.8 %multiply_reduce_fusion.3 = (f32[4,512]{1,0:T(4,128)S(1)}, f32[4,512,2048]{2,1,0:T(8,128)}) fusion(f32[4,512,2048]{2,1,0:T(8,128)} %copy-done.1, f32[4,512]{1,0:T(4,128)S(1)} %dynamic-slice_bitcast_fusion.2, pred[512,2048]{1,0:T(8,128)(4,1)S(1)} %fusion.149, bf16[2048,4,64]{0,2,1:T(8,128)(2,1)} %get-tuple-element.557, ...), kind=kOutput, calls=%fused_computation.19.clone.1 | convolution fusion | flops 557840384 | bytes 35930116 | tf_op jit(solution)/shard_map/while/body/eval_jaxpr/while/body/eval_jaxpr/qhd,khd->hqk/dot_general | solution.py:83
  676.3 12.1 %multiply_convert_fusion.7 = bf16[4,512,2048]{2,1,0:T(8,128)(2,1)S(1)} fusion(f32[4,512,2048]{2,1,0:T(8,128)} %get-tuple-element.477, f32[4,512,2048]{2,1,0:T(8,128)} %copy-done.1, f32[4,512]{1,0:T(4,128)S(1)} %get-tuple-element.478, f32[4,512]{1,0:T(4,128)S(1)} %dynamic-slice_bitcast_fusion.2, pred[512,2048]{1,0:T(8,128)(4,1)S(1)} %fusion.149), kind=kLoop, calls=%fused_computation.18.clone.1 | loop fusion | flops 25165824 | bytes 43008000 | tf_op jit(solution)/shard_map/while/body/eval_jaxpr/while/body/eval_jaxpr/convert_element_type | solution.py:88
  691.1 4.7 fusion.150
  696.3 11.1 %dynamic_update_slice.31 = f32[4,512,4,64]{1,0,3,2:T(4,128)} dynamic-update-slice(f32[4,512,4,64]{1,0,3,2:T(4,128)} %get-tuple-element.534, f32[1,512,4,64]{1,0,3,2:T(1,128)S(1)} %copy.97, s32[]{:T(128)S(6)} %copy.123, s32[]{:T(128)} %constant.124.clone.1..sunk.1, s32[]{:T(128)} %constant.124.clone.1..sunk.1, s32[]{:T(128)} %constant.124.clone.1..sunk.1) | dynamic-update-slice | bytes 1048580 | tf_op jit(solution)/shard_map/while/body/eval_jaxpr/while/body/jit(dynamic_update_index_in_dim)/dynamic_update_slice | solution.py:69
  712.0 3.3 fusion.148
  715.4 5.7 copy-done.1
  721.1 7.5 fusion.151
  728.7 12.8 %multiply_reduce_fusion.3 = (f32[4,512]{1,0:T(4,128)S(1)}, f32[4,512,2048]{2,1,0:T(8,128)}) fusion(f32[4,512,2048]{2,1,0:T(8,128)} %copy-done.1, f32[4,512]{1,0:T(4,128)S(1)} %dynamic-slice_bitcast_fusion.2, pred[512,2048]{1,0:T(8,128)(4,1)S(1)} %fusion.149, bf16[2048,4,64]{0,2,1:T(8,128)(2,1)} %get-tuple-element.557, ...), kind=kOutput, calls=%fused_computation.19.clone.1 | convolution fusion | flops 557840384 | bytes 35930116 | tf_op jit(solution)/shard_map/while/body/eval_jaxpr/while/body/eval_jaxpr/qhd,khd->hqk/dot_general | solution.py:83
  741.5 12.1 %multiply_convert_fusion.7 = bf16[4,512,2048]{2,1,0:T(8,128)(2,1)S(1)} fusion(f32[4,512,2048]{2,1,0:T(8,128)} %get-tuple-element.477, f32[4,512,2048]{2,1,0:T(8,128)} %copy-done.1, f32[4,512]{1,0:T(4,128)S(1)} %get-tuple-element.478, f32[4,512]{1,0:T(4,128)S(1)} %dynamic-slice_bitcast_fusion.2, pred[512,2048]{1,0:T(8,128)(4,1)S(1)} %fusion.149), kind=kLoop, calls=%fused_computation.18.clone.1 | loop fusion | flops 25165824 | bytes 43008000 | tf_op jit(solution)/shard_map/while/body/eval_jaxpr/while/body/eval_jaxpr/convert_element_type | solution.py:88
  756.2 4.7 fusion.150
  761.4 11.1 %dynamic_update_slice.31 = f32[4,512,4,64]{1,0,3,2:T(4,128)} dynamic-update-slice(f32[4,512,4,64]{1,0,3,2:T(4,128)} %get-tuple-element.534, f32[1,512,4,64]{1,0,3,2:T(1,128)S(1)} %copy.97, s32[]{:T(128)S(6)} %copy.123, s32[]{:T(128)} %constant.124.clone.1..sunk.1, s32[]{:T(128)} %constant.124.clone.1..sunk.1, s32[]{:T(128)} %constant.124.clone.1..sunk.1) | dynamic-update-slice | bytes 1048580 | tf_op jit(solution)/shard_map/while/body/eval_jaxpr/while/body/jit(dynamic_update_index_in_dim)/dynamic_update_slice | solution.py:69
  781.4 3.5 fusion.77
  788.9 7.2 convert_bitcast_fusion
  796.2 7.2 convolution_convert_fusion
  816.9 3.4 convert_element_type.236
  821.6 35.0 %all-reduce.6.cloned.1.call-done = (bf16[1024,256]{1,0:T(8,128)(2,1)}, bf16[1024,256]{1,0:T(8,128)(2,1)}, bf16[1024,256]{1,0:T(8,128)(2,1)}, bf16[256,1024]{1,0:T(8,128)(2,1)}) async-done(((bf16[1024,256]{1,0:T(8,128)(2,1)}, bf16[1024,256]{1,0:T(8,128)(2,1)}, bf16[1024,256]{1,0:T(8,128)(2,1)}, bf16[256,1024]{1,0:T(8,128)(2,1)}), (bf16[1024,256]{1,0:T(8,128)(2,1)}, bf16[1024,256]{1,0:T(8,128)(2,1)}, ...) | async-done | bytes 2097168 | tf_op jit(solution)/shard_map/psum | solution.py:258
  865.9 45.2 %all-reduce = (f32[1024]{0:T(1024)}, f32[1024]{0:T(1024)}, f32[2]{0:T(128)}) all-reduce(f32[1024]{0:T(1024)} %get-tuple-element.261, f32[1024]{0:T(1024)} %get-tuple-element.259, f32[2]{0:T(128)} %pad_maximum_fusion.7), channel_id=1, replica_groups=mesh['dp'=2,'head'=4,'mlp'=4] {'dp','head','mlp'}, use_global_device_ids=true, to_apply=%region_16.17 | all-reduce | flops 2050 | bytes 16400 | tf_op jit(solution)/shard_map/psum | solution.py:276
  913.5 17.4 %reduce-scatter.7.cloned.1.call-done = bf16[512,1,1024]{2,0,1:T(8,128)(2,1)} async-done(((bf16[512,4,1024]{2,0,1:T(8,128)(2,1)}), bf16[512,1,1024]{2,0,1:T(8,128)(2,1)}) %reduce-scatter.7.cloned.1.call-update) | async-done | bytes 1048592 | tf_op jit(solution)/shard_map/reduce_scatter | solution.py:193
  930.9 4.4 fusion.66
  (240 shorter events, 135.8 us)
Async XLA Ops:
  8.0 340.5 %copy-start = (bf16[704,1024]{1,0:T(8,128)(2,1)S(1)}, bf16[704,1024]{1,0:T(8,128)(2,1)}, u32[]{:S(2)}) copy-start(bf16[704,1024]{1,0:T(8,128)(2,1)} %param.30) | copy-start | bytes 4325380
  8.0 4.9 copy-start.39
  8.0 4.9 copy-start.21
  8.0 60.4 %all-gather.4.cloned.1.call-start = ((), (), s32[]{:S(2)}) async-start(), calls=%async_computation.4 | async-start | bytes 5242880 | tf_op jit(solution)/shard_map/all_gather | solution.py:137
  12.9 229.6 %reduce-scatter.5.cloned.1.call-start = ((), (), s32[]{:S(2)}) async-start(), calls=%async_computation.5 | async-start | bytes 10485760 | tf_op jit(solution)/shard_map/reduce_scatter | solution.py:169
  16.9 1.1 copy-start.29
  19.8 58.2 %copy-start.13 = (f32[2048,32]{0,1:T(8,128)}, f32[2048,32]{0,1:T(8,128)S(1)}, u32[]{:S(2)}) copy-start(f32[2048,32]{0,1:T(8,128)S(1)} %get-tuple-element.348) | copy-start | bytes 786436
  85.2 5.0 copy-start.22
  95.6 1.0 copy-start.23
  102.2 5.0 copy-start.22
  112.6 1.0 copy-start.23
  119.2 5.0 copy-start.22
  129.6 1.0 copy-start.23
  136.2 5.0 copy-start.22
  146.7 1.0 copy-start.23
  147.6 8.3 copy-start.4
  147.6 3.7 copy-start.25
  150.3 1.0 copy-start.9
  155.9 86.6 %copy-start.2 = (bf16[512,1,1024]{2,0,1:T(8,128)(2,1)S(1)}, bf16[512,1,1024]{2,0,1:T(8,128)(2,1)}, u32[]{:S(2)}) copy-start(bf16[512,1,1024]{2,0,1:T(8,128)(2,1)} %param.18) | copy-start | bytes 3145732
  155.9 192.6 %all-gather.6.cloned.1.call-start = ((), (), s32[]{:S(2)}) async-start(), calls=%async_computation.7 | async-start | bytes 5242880 | tf_op jit(solution)/shard_map/all_gather | solution.py:197
  156.5 89.2 %copy-start.30 = (f32[1024]{0:T(1024)S(1)}, f32[1024]{0:T(1024)}, u32[]{:S(2)}) copy-start(f32[1024]{0:T(1024)} %param.27) | copy-start | bytes 12292
  156.5 288.7 %reduce-scatter.9.cloned.1.call-start = ((), (), s32[]{:S(2)}) async-start(), calls=%async_computation.8 | async-start | bytes 5242880 | tf_op jit(solution)/shard_map/reduce_scatter | solution.py:212
  245.7 202.7 %copy-start.33 = (f32[512]{0:T(512)}, f32[512]{0:T(512)S(1)}, u32[]{:S(2)}) copy-start(f32[512]{0:T(512)S(1)} %add_rsqrt_fusion) | copy-start | bytes 6148
  247.6 26.7 %collective-permute-start = (bf16[512,1,1024]{2,0,1:T(8,128)(2,1)S(1)}, bf16[512,1,1024]{2,0,1:T(8,128)(2,1)S(1)}, u32[]{:S(2)}, u32[]{:S(2)}) collective-permute-start(bf16[512,1,1024]{2,0,1:T(8,128)(2,1)S(1)} %multiply_convert_fusion.5), channel_id=1, source_target_pairs={{0,1},{1,2},{2,3},{3,0},{4,5},{5,6},{6,7},{7,4},{8,9},{9,10},{10,1... | collective-permute-start | bytes 3145736 | tf_op jit(solution)/shard_map/ppermute | solution.py:181
  274.3 25.9 %collective-permute-start.1 = (bf16[512,1,1024]{2,0,1:T(8,128)(2,1)S(1)}, bf16[512,1,1024]{2,0,1:T(8,128)(2,1)}, u32[]{:S(2)}, u32[]{:S(2)}) collective-permute-start(bf16[512,1,1024]{2,0,1:T(8,128)(2,1)S(1)} %collective-permute-done), channel_id=1, source_target_pairs={{0,1},{1,2},{2,3},{3,0},{4,5},{5,6},{6,7},{7,4},{8,9},{9,10},{10,1... | collective-permute-start | bytes 3145736 | tf_op jit(solution)/shard_map/ppermute | solution.py:181
  300.2 25.2 %collective-permute-start.2 = (bf16[512,1,1024]{2,0,1:T(8,128)(2,1)}, bf16[512,1,1024]{2,0,1:T(8,128)(2,1)}, u32[]{:S(2)}, u32[]{:S(2)}) collective-permute-start(bf16[512,1,1024]{2,0,1:T(8,128)(2,1)} %collective-permute-done.1), channel_id=1, source_target_pairs={{0,1},{1,2},{2,3},{3,0},{4,5},{5,6},{6,7},{7,4},{8,9},{9,10},{10,1... | collective-permute-start | bytes 3145736 | tf_op jit(solution)/shard_map/ppermute | solution.py:181
  332.5 5.3 copy-start.16
  332.5 5.3 copy-start.18
  334.6 3.2 copy-start.32
  348.5 13.1 %copy-start.17 = (bf16[1024,704]{1,0:T(8,128)(2,1)S(1)}, bf16[1024,704]{1,0:T(8,128)(2,1)}, u32[]{:S(2)}) copy-start(bf16[1024,704]{1,0:T(8,128)(2,1)} %copy.68) | copy-start | bytes 4325380
  348.5 13.1 %copy-start.19 = (bf16[1024,704]{1,0:T(8,128)(2,1)S(1)}, bf16[1024,704]{1,0:T(8,128)(2,1)}, u32[]{:S(2)}) copy-start(bf16[1024,704]{1,0:T(8,128)(2,1)} %copy.69) | copy-start | bytes 4325380
  359.1 1.6 copy-start.44
  359.1 2.5 copy-start.45
  371.0 78.0 %copy-start.5 = (bf16[512,1,1024]{2,0,1:T(8,128)(2,1)S(1)}, bf16[512,1,1024]{2,0,1:T(8,128)(2,1)}, u32[]{:S(2)}) copy-start(bf16[512,1,1024]{2,0,1:T(8,128)(2,1)} %param.31) | copy-start | bytes 3145732
  371.1 136.8 %all-gather.8.cloned.1.call-start = ((), (), s32[]{:S(2)}) async-start(), calls=%async_computation.9 | async-start | bytes 5242880 | tf_op jit(solution)/shard_map/all_gather | solution.py:218
  445.2 3.9 copy-start.7
  452.4 359.4 %all-reduce.8.cloned.1.call-start = ((), (), s32[]{:S(2)}) async-start(), calls=%async_computation.12 | async-start | bytes 9175040 | tf_op jit(solution)/shard_map/psum | solution.py:268
  452.5 12.8 %copy-start.43 = (bf16[512,4,704]{0,2,1:T(8,128)(2,1)S(1)}, bf16[512,4,704]{0,2,1:T(8,128)(2,1)}, u32[]{:S(2)}) copy-start(bf16[512,4,704]{0,2,1:T(8,128)(2,1)} %get-tuple-element.321) | copy-start | bytes 8650756
  462.9 3.3 copy-start.42
  470.5 37.3 %copy-start.26 = (bf16[256,1024]{1,0:T(8,128)(2,1)S(1)}, bf16[256,1024]{1,0:T(8,128)(2,1)}, u32[]{:S(2)}) copy-start(bf16[256,1024]{1,0:T(8,128)(2,1)} %param.26) | copy-start | bytes 1572868
  470.5 386.0 %all-reduce.6.cloned.1.call-start = ((), (), s32[]{:S(2)}) async-start(), calls=%async_computation.11 | async-start | bytes 4194304 | tf_op jit(solution)/shard_map/psum | solution.py:258
  520.5 6.0 copy-start.1
  585.0 5.8 copy-start.1
  650.2 5.8 copy-start.1
  715.4 5.8 copy-start.1
  778.0 2.0 copy-start.14
  778.1 3.3 copy-start.40
  778.2 6.7 copy-start.24
  780.1 8.8 copy-start.11
  781.4 4.7 copy-start.41
  784.9 1.8 copy-start.10
  788.8 74.4 %reduce-scatter.11.cloned.1.call-start = ((), (), s32[]{:S(2)}) async-start(), calls=%async_computation.10 | async-start | bytes 5242880 | tf_op jit(solution)/shard_map/reduce_scatter | solution.py:247
  796.1 134.8 %reduce-scatter.7.cloned.1.call-start = ((), (), s32[]{:S(2)}) async-start(), calls=%async_computation.6 | async-start | bytes 5242880 | tf_op jit(solution)/shard_map/reduce_scatter | solution.py:193
  803.3 3.0 copy-start.8
  811.8 3.1 copy-start.15
  816.9 3.4 copy-start.12
  856.6 4.5 copy-start.28
  856.6 5.5 copy-start.27
  856.6 6.6 copy-start.3
  856.6 6.6 copy-start.35
  856.6 6.6 copy-start.37
  861.0 69.9 %copy-start.6 = (bf16[512,1,1024]{2,0,1:T(8,128)(2,1)S(1)}, bf16[512,1,1024]{2,0,1:T(8,128)(2,1)}, u32[]{:S(2)}) copy-start(bf16[512,1,1024]{2,0,1:T(8,128)(2,1)} %param.31) | copy-start | bytes 3145732
  861.0 69.9 %copy-start.31 = (f32[1024]{0:T(1024)S(1)}, f32[1024]{0:T(1024)}, u32[]{:S(2)}) copy-start(f32[1024]{0:T(1024)} %param.27) | copy-start | bytes 12292
  861.0 69.9 %copy-start.34 = (f32[512]{0:T(512)S(1)}, f32[512]{0:T(512)}, u32[]{:S(2)}) copy-start(f32[512]{0:T(512)} %copy-done.33) | copy-start | bytes 6148
  (3 other events, 1.9 us)
Sparse Core Ops, SparseCore 0:
  13.0 55.3 all-gather.3
  156.0 86.4 reduce-scatter.4
  452.5 55.2 all-gather.7
  796.2 54.5 reduce-scatter.10
  853.1 77.7 reduce-scatter.6
Sparse Core Ops, SparseCore 1:
  158.0 80.6 all-gather.5
  371.1 74.0 reduce-scatter.8
  470.6 108.2 all-reduce.7
  788.9 67.6 all-reduce.5
